TPU v7x, 512 devices: a whole 4x8x8 slice. The times are simulated.
512 devices in a mesh: graph: 16 (over z, core), config: 32 (over y, x).
Axes of the slice: x: 4, y: 8, z: 8, core: 2. Of those that a mesh axis runs over, the one named last changes fastest.
Arguments:
- features: bfloat16 [64, 8192, 128], P('config', 'graph'), may hold values from -6 to 6
- cotangent: bfloat16 [64, 8192, 128], P(None, ('graph', 'config')), may hold values from -6 to 6
- sage_weight: bfloat16 [2, 128, 128], replicated, may hold values from -0.5 to 0.5
- attn_weight: bfloat16 [4, 128, 128], replicated, may hold values from -0.5 to 0.5
- tile_vals: bfloat16 [192, 128, 128], P('graph'), may hold values from -0.375 to 0.375
- tile_dst: int32 [192], P('graph'), may hold values from 0 to 3
- tile_src: int32 [192], P('graph'), may hold values from 0 to 3
- tile_count: int32 [16], P('graph'), may hold values from 3 to 12, as said below
- hub_ids: int32 [128], P('graph'), may hold values from 0 to 8191, as said below
- hub_weight: bfloat16 [8192, 128], P('graph'), may hold values from -0.5 to 0.5
Outputs:
- layer_out: bfloat16 [64, 8192, 128], P(None, ('graph', 'config'))
- grad_features: bfloat16 [64, 8192, 128], P('config', 'graph')
- grad_weights: float32 [16, 6, 128, 128], P('graph')
Inputs may be any that keep to these rules, and one draw needn't show every extreme that they name: Slot t of slab g (t counted within the slab) is live when t < tile_count[g]; some slab has all 12 slots live. `hub_ids`: entries g * 8 to (g+1) * 8 - 1 are distinct nodes of slab g.
All inputs are finite; a program needn't handle non-finite values.
Results may differ from a plain program's by a relative error of at most 0.024.
Values may be sent and summed in bfloat16 or wider, within the bound.
A program may use at most 64 MiB of HBM per device.

v0:
```python
import math
import jax
import jax.numpy as jnp
from jax import lax
from jax.sharding import PartitionSpec as P

HEADS = 4
CAP = 20.0


def attend(queries, key_rows, value_rows):
    layout_count, node_count, feature_width = queries.shape
    head_size = feature_width // HEADS
    split = (layout_count, node_count, HEADS, head_size)
    query_b = queries.reshape(split)
    key_b = key_rows.reshape(split)
    value_b = value_rows.reshape(split)
    scores = jnp.einsum(
        "lkhd,mkhd->khlm", query_b, key_b, preferred_element_type=jnp.float32
    ) / math.sqrt(head_size)
    capped = CAP * jnp.tanh(scores / CAP)
    weights = jnp.exp(capped)
    attention = weights / jnp.sum(weights, axis=-1, keepdims=True)
    attention = attention.astype(value_b.dtype)
    mixture = jnp.einsum("khlm,mkhd->lkhd", attention, value_b, preferred_element_type=jnp.float32)
    return mixture.reshape(layout_count, node_count, feature_width).astype(queries.dtype)


def project(flat_rows, weight):
    return jnp.dot(flat_rows, weight, preferred_element_type=jnp.float32)


def project_back(flat_rows, weight):
    return jnp.dot(flat_rows, weight.T, preferred_element_type=jnp.float32)


def outer_sum(left_rows, right_rows):
    return jnp.dot(left_rows.T, right_rows, preferred_element_type=jnp.float32)


def sage_forward(feats, aggregate, sage_weight):
    shaped = feats.shape
    width_f = shaped[-1]
    pre_acts = project(feats.reshape(-1, width_f), sage_weight[0]) + project(
        aggregate.reshape(-1, width_f), sage_weight[1]
    )
    hidden = jax.nn.silu(pre_acts).astype(jnp.bfloat16)
    return (pre_acts.reshape(shaped), hidden.reshape(shaped))


def node_forward(hidden, attn_weight):
    shaped = hidden.shape
    width_f = shaped[-1]
    three = (shaped[0], -1, width_f)
    flat_hidden = hidden.reshape(-1, width_f)
    queries = project(flat_hidden, attn_weight[0]).astype(jnp.bfloat16)
    key_rows = project(flat_hidden, attn_weight[1]).astype(jnp.bfloat16)
    value_rows = project(flat_hidden, attn_weight[2]).astype(jnp.bfloat16)
    mixture = attend(queries.reshape(three), key_rows.reshape(three), value_rows.reshape(three))
    output = (
        flat_hidden.astype(jnp.float32) + project(mixture.reshape(-1, width_f), attn_weight[3])
    ).astype(jnp.bfloat16)
    return (
        output.reshape(shaped),
        queries.reshape(shaped),
        key_rows.reshape(shaped),
        value_rows.reshape(shaped),
        mixture.reshape(shaped),
    )


def node_backward(cot_rows, hidden, queries, key_rows, value_rows, mixture, attn_weight):
    shaped = hidden.shape
    width_f = shaped[-1]
    three = (shaped[0], -1, width_f)
    flat_cot = cot_rows.reshape(-1, width_f)
    grad_mix = project_back(flat_cot, attn_weight[3]).astype(jnp.bfloat16)
    grad_wo = outer_sum(mixture.reshape(-1, width_f), flat_cot)
    unused, pullback = jax.vjp(attend, queries, key_rows, value_rows)
    grad_q, grad_k, grad_v = pullback(grad_mix.reshape(three))
    flat_q = grad_q.reshape(-1, width_f)
    flat_k = grad_k.reshape(-1, width_f)
    flat_v = grad_v.reshape(-1, width_f)
    grad_hidden = (
        flat_cot.astype(jnp.float32)
        + project_back(flat_q, attn_weight[0])
        + project_back(flat_k, attn_weight[1])
        + project_back(flat_v, attn_weight[2])
    ).astype(jnp.bfloat16)
    flat_hidden = hidden.reshape(-1, width_f)
    grads = jnp.stack(
        [
            outer_sum(flat_hidden, flat_q),
            outer_sum(flat_hidden, flat_k),
            outer_sum(flat_hidden, flat_v),
            grad_wo,
        ]
    )
    return (grad_hidden.reshape(shaped), grads)


def sage_backward(grad_hidden, pre_acts, feats, aggregate, sage_weight):
    shaped = feats.shape
    width_f = shaped[-1]
    flat_pre = pre_acts.reshape(-1, width_f)
    sigmoid_pre = jax.nn.sigmoid(flat_pre)
    grad_pre = (
        grad_hidden.reshape(-1, width_f).astype(jnp.float32)
        * sigmoid_pre
        * (1.0 + flat_pre * (1.0 - sigmoid_pre))
    ).astype(jnp.bfloat16)
    grads = jnp.stack(
        [
            outer_sum(feats.reshape(-1, width_f), grad_pre),
            outer_sum(aggregate.reshape(-1, width_f), grad_pre),
        ]
    )
    grad_self = project_back(grad_pre, sage_weight[0]).astype(jnp.bfloat16).reshape(shaped)
    grad_agg = project_back(grad_pre, sage_weight[1]).astype(jnp.bfloat16).reshape(shaped)
    return (grad_self, grad_agg, grads)


def tile_forward(source, tile_vals, tile_src, tile_dst, live):
    layout_count, node_count, width_f = source.shape
    tile_size = tile_vals.shape[1]
    block_count = node_count // tile_size
    blocks = source.reshape(layout_count, block_count, tile_size, width_f)[:, tile_src]
    products = jnp.einsum("tij,ltjf->tlif", tile_vals, blocks, preferred_element_type=jnp.float32)
    products = products * live[:, None, None, None]
    summed = jax.ops.segment_sum(products, tile_dst, num_segments=block_count)
    return summed.transpose(1, 0, 2, 3).reshape(layout_count, node_count, width_f)


def tile_backward(grad_agg, tile_vals, tile_dst, tile_src, live):
    layout_count, node_count, width_f = grad_agg.shape
    tile_size = tile_vals.shape[1]
    block_count = node_count // tile_size
    blocks = grad_agg.reshape(layout_count, block_count, tile_size, width_f)[:, tile_dst]
    products = jnp.einsum("tij,ltif->tljf", tile_vals, blocks, preferred_element_type=jnp.float32)
    products = products * live[:, None, None, None]
    summed = jax.ops.segment_sum(products, tile_src, num_segments=block_count)
    return summed.transpose(1, 0, 2, 3).reshape(layout_count, node_count, width_f)


def flatten_nodes(arrays):
    return tuple((item.reshape(item.shape[0], -1, item.shape[-1]) for item in arrays))


def local(
    features,
    cotangent,
    sage_weight,
    attn_weight,
    tile_vals,
    tile_dst,
    tile_src,
    tile_count,
    hub_ids,
    hub_weight,
):
    layout_dev, node_dev, width_f = features.shape
    config_count = lax.axis_size("config")
    node_share = node_dev // config_count
    slab_index = lax.axis_index("graph")
    hub_local = hub_ids - slab_index * node_dev
    live = (jnp.arange(tile_dst.shape[0], dtype=jnp.int32) < tile_count[0]).astype(jnp.float32)
    local_hubs = features[:, hub_local]
    columns = hub_weight
    hub_sum = jnp.einsum(
        "nj,ljf->lnf",
        columns,
        lax.all_gather(local_hubs, "graph", axis=1, tiled=True),
        preferred_element_type=jnp.float32,
    )
    aggregate = (tile_forward(features, tile_vals, tile_src, tile_dst, live) + hub_sum).astype(
        jnp.bfloat16
    )
    split_shape = (layout_dev, config_count, node_share, width_f)
    back_shape = (layout_dev * config_count, 1, node_share, width_f)
    received = (
        lax.all_to_all(
            features.reshape(split_shape), "config", split_axis=1, concat_axis=0, tiled=True
        ),
        lax.all_to_all(
            aggregate.reshape(split_shape), "config", split_axis=1, concat_axis=0, tiled=True
        ),
    )
    pre_in, hidden_in = sage_forward(received[0], received[1], sage_weight)
    results = (received[0], received[1], pre_in, hidden_in) + node_forward(hidden_in, attn_weight)
    feats_node, agg_node, pre_node, hidden_node, output, queries, key_rows, value_rows, mixture = (
        flatten_nodes(results)
    )
    grad_hidden, attn_grads = node_backward(
        cotangent, hidden_node, queries, key_rows, value_rows, mixture, attn_weight
    )
    self_node, aggr_node, sage_grads = sage_backward(
        grad_hidden, pre_node, feats_node, agg_node, sage_weight
    )
    self_back, agg_back = (
        lax.all_to_all(
            self_node.reshape(back_shape), "config", split_axis=0, concat_axis=1, tiled=True
        ),
        lax.all_to_all(
            aggr_node.reshape(back_shape), "config", split_axis=0, concat_axis=1, tiled=True
        ),
    )
    grad_self = self_back.reshape(layout_dev, node_dev, width_f)
    grad_agg = agg_back.reshape(layout_dev, node_dev, width_f)
    back_rows = tile_backward(grad_agg, tile_vals, tile_dst, tile_src, live)
    columns = hub_weight
    hub_grads = lax.psum_scatter(
        jnp.einsum("nj,lnf->jlf", columns, grad_agg, preferred_element_type=jnp.float32).astype(
            jnp.bfloat16
        ),
        "graph",
        scatter_dimension=0,
        tiled=True,
    ).astype(jnp.float32)
    totals = grad_self.astype(jnp.float32) + back_rows
    totals = totals.at[:, hub_local].add(jnp.transpose(hub_grads, (1, 0, 2)))
    grad_features = totals.astype(jnp.bfloat16)
    partial_grads = jnp.concatenate([sage_grads, attn_grads], axis=0)
    summed = lax.psum(partial_grads.astype(jnp.bfloat16), "config").astype(jnp.float32)
    scale = 1.0 / math.sqrt(layout_dev * config_count * node_dev)
    return (output, grad_features, (summed * scale)[None])


def solution(mesh):
    return jax.shard_map(
        local,
        mesh=mesh,
        in_specs=(
            P("config", "graph", None),
            P(None, ("graph", "config"), None),
            P(),
            P(),
            P("graph", None, None),
            P("graph"),
            P("graph"),
            P("graph"),
            P("graph"),
            P("graph", None),
        ),
        out_specs=(
            P(None, ("graph", "config"), None),
            P("config", "graph", None),
            P("graph", None, None, None),
        ),
        check_vma=False,
    )
```

profile of v0, /device:TPU:1, one launch (start us, length us, event | category | flops | bytes accessed | tf_op | source)
XLA Modules:
  0.0 400.2 jit_solution(9092489679401032103)
XLA Ops:
  8.0 1.7 copy.116
  9.7 10.5 %all-to-all-start = ((bf16[2,32,16,128]{3,2,0,1:T(8,128)(2,1)}), bf16[2,32,16,128]{3,2,0,1:T(8,128)(2,1)S(1)}, u32[]{:S(2)}, u32[]{:S(2)}) async-start(bf16[2,32,16,128]{3,2,0,1:T(8,128)(2,1)} %copy.116), calls=%async_computation | async-start | bytes 524288 | tf_op jit(solution)/shard_map/all_to_all | solution.py:181
  20.2 0.7 compare_select_fusion
  20.9 0.7 compare_select_fusion.1
  21.6 1.5 gather_fusion.1
  23.8 0.7 compare_select_fusion.2
  24.4 1.6 gather_fusion
  26.1 1.6 multiply_bitcast_fusion.1
  27.7 1.9 copy.118
  29.6 1.8 scatter_fusion
  32.0 24.1 %all-gather = bf16[2,128,128]{2,1,0:T(8,128)(2,1)S(1)} all-gather(bf16[2,8,128]{2,1,0:T(8,128)(2,1)S(1)} %bitcast.206), channel_id=2, replica_groups=mesh['graph'=16,'config'=32] {'graph'}, dimensions={1}, use_global_device_ids=true | all-gather | bytes 69632 | tf_op jit(solution)/shard_map/all_gather | solution.py:172
  56.5 0.7 copy.121
  57.2 9.8 %all-to-all-start.1 = ((bf16[2,32,16,128]{3,2,0,1:T(8,128)(2,1)}), bf16[2,32,16,128]{3,2,0,1:T(8,128)(2,1)S(1)}, u32[]{:S(2)}, u32[]{:S(2)}) async-start(bf16[2,32,16,128]{3,2,0,1:T(8,128)(2,1)} %copy.121), calls=%async_computation.1 | async-start | bytes 524288 | tf_op jit(solution)/shard_map/all_to_all | solution.py:184
  67.3 0.4 reshape.85
  67.7 1.2 copy.127
  68.9 1.3 dynamic-slice
  71.1 7.6 %all-to-all-done.1 = bf16[2,32,16,128]{3,2,0,1:T(8,128)(2,1)S(1)} async-done(((bf16[2,32,16,128]{3,2,0,1:T(8,128)(2,1)}), bf16[2,32,16,128]{3,2,0,1:T(8,128)(2,1)S(1)}, u32[]{:S(2)}, u32[]{:S(2)}) %all-to-all-start.1) | async-done | bytes 262176 | tf_op jit(solution)/shard_map/all_to_all | solution.py:184
  78.7 1.1 multiply_convert_fusion
  80.0 0.9 convolution_convert_fusion.8
  81.1 0.4 reshape_reshape.24
  81.5 1.2 copy.122
  82.7 2.1 reshape_reshape.25
  84.8 1.8 copy.123
  86.6 3.2 fusion.7
  89.8 0.6 copy-done.15
  90.5 0.6 multiply_divide_fusion
  91.5 1.9 copy.124
  93.4 2.8 fusion.6
  96.2 1.0 fusion.4
  97.2 1.5 fusion.9
  98.7 1.2 fusion.8
  99.9 1.5 fusion.10
  101.8 1.6 copy.134
  103.5 0.5 reshape.87
  104.0 2.5 copy.131
  106.5 0.5 reshape.86
  107.0 1.0 convolution_add_fusion.2
  108.1 2.5 copy.137
  110.6 1.2 reshape.88
  111.8 1.3 convolution_add_fusion.1
  113.1 1.5 fusion.18
  114.9 0.9 convolution_convert_fusion.5
  117.0 4.4 %all-to-all-start.3 = ((bf16[64,1,16,128]{3,2,1,0:T(8,128)(2,1)}), bf16[64,1,16,128]{3,2,1,0:T(8,128)(2,1)S(1)}, u32[]{:S(2)}, u32[]{:S(2)}) async-start(bf16[64,1,16,128]{3,2,1,0:T(8,128)(2,1)} %bitcast.37), calls=%async_computation.3 | async-start | bytes 524288 | tf_op jit(solution)/shard_map/all_to_all | solution.py:203
  121.8 0.7 copy-done.12
  122.6 1.6 copy.126
  124.2 0.5 convert_element_type.128
  124.7 1.7 fusion.13
  126.4 0.9 convolution_convert_fusion.6
  127.3 4.5 %all-to-all-done.3 = bf16[64,1,16,128]{3,2,1,0:T(8,128)(2,1)S(1)} async-done(((bf16[64,1,16,128]{3,2,1,0:T(8,128)(2,1)}), bf16[64,1,16,128]{3,2,1,0:T(8,128)(2,1)S(1)}, u32[]{:S(2)}, u32[]{:S(2)}) %all-to-all-start.3) | async-done | bytes 262176 | tf_op jit(solution)/shard_map/all_to_all | solution.py:203
  131.8 5.2 %all-to-all-start.2 = ((bf16[64,1,16,128]{3,2,1,0:T(8,128)(2,1)}), bf16[64,1,16,128]{3,2,1,0:T(8,128)(2,1)S(1)}, u32[]{:S(2)}, u32[]{:S(2)}) async-start(bf16[64,1,16,128]{3,2,1,0:T(8,128)(2,1)} %bitcast.32), calls=%async_computation.2 | async-start | bytes 524288 | tf_op jit(solution)/shard_map/all_to_all | solution.py:200
  137.1 136.0 %all-reduce.4.cloned.1.call-done = bf16[6,128,128]{1,2,0:T(8,128)(2,1)} async-done(((bf16[6,128,128]{1,2,0:T(8,128)(2,1)}), bf16[6,128,128]{1,2,0:T(8,128)(2,1)}) %all-reduce.4.cloned.1.call-update) | async-done | bytes 196624 | tf_op jit(solution)/shard_map/psum | solution.py:223
  273.1 1.0 multiply_bitcast_fusion.2
  274.1 0.9 copy.157
  275.0 0.7 gather_fusion.2
  275.7 1.6 multiply_bitcast_fusion
  277.3 1.9 copy.143
  279.3 1.8 scatter_fusion.1
  281.4 1.2 fusion.19
  282.5 0.8 copy.148
  283.3 0.6 bitcast_add_fusion
  283.9 106.4 %all-reduce.6.cloned.1.call-done = bf16[128,2,128]{2,1,0:T(2,128)(2,1)} async-done(((bf16[128,2,128]{2,1,0:T(2,128)(2,1)}), bf16[128,2,128]{2,1,0:T(2,128)(2,1)}) %all-reduce.6.cloned.1.call-update) | async-done | bytes 65552
  390.3 0.7 dynamic-slice_convert_fusion
  391.0 0.8 scatter_fusion.2
  392.0 0.7 copy.156
  (68 shorter events, 5.1 us)
Async XLA Ops:
  8.0 18.1 %copy-start = (bf16[12,128,128]{2,1,0:T(8,128)(2,1)S(1)}, bf16[12,128,128]{2,1,0:T(8,128)(2,1)}, u32[]{:S(2)}) copy-start(bf16[12,128,128]{2,1,0:T(8,128)(2,1)} %param.14) | copy-start | bytes 1179652
  9.7 47.5 %all-to-all-start = ((bf16[2,32,16,128]{3,2,0,1:T(8,128)(2,1)}), bf16[2,32,16,128]{3,2,0,1:T(8,128)(2,1)S(1)}, u32[]{:S(2)}, u32[]{:S(2)}) async-start(bf16[2,32,16,128]{3,2,0,1:T(8,128)(2,1)} %copy.116), calls=%async_computation | async-start | bytes 524288 | tf_op jit(solution)/shard_map/all_to_all | solution.py:181
  27.7 1.9 copy-start.17
  31.5 24.6 %copy-start.9 = (bf16[512,128]{1,0:T(8,128)(2,1)S(1)}, bf16[512,128]{1,0:T(8,128)(2,1)}, u32[]{:S(2)}) copy-start(bf16[512,128]{1,0:T(8,128)(2,1)} %param.19) | copy-start | bytes 393220
  31.7 35.3 %copy-start.1 = (bf16[64,16,128]{2,1,0:T(8,128)(2,1)S(1)}, bf16[64,16,128]{2,1,0:T(8,128)(2,1)}, u32[]{:S(2)}) copy-start(bf16[64,16,128]{2,1,0:T(8,128)(2,1)} %param.11) | copy-start | bytes 786436
  31.7 35.3 %copy-start.10 = (bf16[4,128,128]{2,1,0:T(8,128)(2,1)S(1)}, bf16[4,128,128]{2,1,0:T(8,128)(2,1)}, u32[]{:S(2)}) copy-start(bf16[4,128,128]{2,1,0:T(8,128)(2,1)} %param.13) | copy-start | bytes 393220
  57.2 13.6 %copy-start.13 = (bf16[2,128,128]{2,1,0:T(8,128)(2,1)S(1)}, bf16[2,128,128]{2,1,0:T(8,128)(2,1)}, u32[]{:S(2)}) copy-start(bf16[2,128,128]{2,1,0:T(8,128)(2,1)} %param.12) | copy-start | bytes 196612
  57.2 21.5 %all-to-all-start.1 = ((bf16[2,32,16,128]{3,2,0,1:T(8,128)(2,1)}), bf16[2,32,16,128]{3,2,0,1:T(8,128)(2,1)S(1)}, u32[]{:S(2)}, u32[]{:S(2)}) async-start(bf16[2,32,16,128]{3,2,0,1:T(8,128)(2,1)} %copy.121), calls=%async_computation.1 | async-start | bytes 524288 | tf_op jit(solution)/shard_map/all_to_all | solution.py:184
  78.7 2.2 copy-start.7
  89.8 0.6 copy-start.15
  93.4 2.9 copy-start.2
  93.4 2.9 copy-start.16
  97.2 1.5 copy-start.3
  98.7 2.7 copy-start.4
  99.9 1.9 copy-start.5
  103.4 3.6 copy-start.11
  113.1 1.8 copy-start.14
  113.1 2.8 copy-start.8
  114.6 2.1 copy-start.6
  117.0 14.8 %all-to-all-start.3 = ((bf16[64,1,16,128]{3,2,1,0:T(8,128)(2,1)}), bf16[64,1,16,128]{3,2,1,0:T(8,128)(2,1)S(1)}, u32[]{:S(2)}, u32[]{:S(2)}) async-start(bf16[64,1,16,128]{3,2,1,0:T(8,128)(2,1)} %bitcast.37), calls=%async_computation.3 | async-start | bytes 524288 | tf_op jit(solution)/shard_map/all_to_all | solution.py:203
  121.4 151.7 %all-reduce.4.cloned.1.call-start = ((), (), s32[]{:S(2)}) async-start(), calls=%async_computation.4 | async-start | bytes 393216 | tf_op jit(solution)/shard_map/psum | solution.py:223
  121.8 0.7 copy-start.12
  131.8 149.3 %all-to-all-start.2 = ((bf16[64,1,16,128]{3,2,1,0:T(8,128)(2,1)}), bf16[64,1,16,128]{3,2,1,0:T(8,128)(2,1)S(1)}, u32[]{:S(2)}, u32[]{:S(2)}) async-start(bf16[64,1,16,128]{3,2,1,0:T(8,128)(2,1)} %bitcast.32), calls=%async_computation.2 | async-start | bytes 524288 | tf_op jit(solution)/shard_map/all_to_all | solution.py:200
  137.0 253.3 %all-reduce.6.cloned.1.call-start = ((), (), s32[]{:S(2)}) async-start(), calls=%async_computation.5 | async-start | bytes 131072
  277.3 1.9 copy-start.18
Sparse Core Ops, SparseCore 0:
  126.0 147.0 all-reduce.3
Sparse Core Ops, SparseCore 1:
  283.4 106.9 all-reduce.5
where the time goes:
time: 401 us; the launch traced here: 400 us
  waiting for transfers between devices  255 us (64%)
  local copies, waits for them, and re-layouts  36.5 us (9%)
  starting transfers between devices  30 us (7%)
  matrix products  27.2 us (7%)
  blocking collectives  24.1 us (6%)
  between operations  17.4 us (4%)
  other arithmetic  10.5 us (3%)
    psum x1, waiting for transfers between devices, local(): lax.psum(partial_grads.astype(jnp.bfloat16), 'config').astype(jnp.float32)  136 us
    unnamed x3, waiting for transfers between devices  106 us
    all_gather x1, blocking collectives, local(): lax.all_gather(local_hubs, 'graph', axis=1, tiled=True)  24.1 us
    all_to_all x1, starting transfers between devices, local(): lax.all_to_all(features.reshape(split_shape), 'config', split_axis=1, con...  10.5 us
    all_to_all x1, starting transfers between devices, local(): lax.all_to_all(aggregate.reshape(split_shape), 'config', split_axis=1, co...  9.81 us
  transfers between devices with their start and end apart: 6, of which 4 were waited for; matrix products, arithmetic and copies ran while one was open for 7% of the time, Pallas kernels for 0%

commit v1 on v0

--- a/solution.py
+++ b/solution.py
@@ -6,6 +6,12 @@
 
 HEADS = 4
 CAP = 20.0
+
+
+def add_all(x, axis):
+    pieces = lax.all_gather(x, axis, axis=0, tiled=False)
+    total = pieces.sum(axis=0)
+    return total
 
 
 def attend(queries, key_rows, value_rows):
@@ -220,7 +226,7 @@
     totals = totals.at[:, hub_local].add(jnp.transpose(hub_grads, (1, 0, 2)))
     grad_features = totals.astype(jnp.bfloat16)
     partial_grads = jnp.concatenate([sage_grads, attn_grads], axis=0)
-    summed = lax.psum(partial_grads.astype(jnp.bfloat16), "config").astype(jnp.float32)
+    summed = add_all(partial_grads.astype(jnp.bfloat16), "config").astype(jnp.float32)
     scale = 1.0 / math.sqrt(layout_dev * config_count * node_dev)
     return (output, grad_features, (summed * scale)[None])
 

time: 401 us -> 253 us (0.63)
  waiting for transfers between devices: 255 us -> 96.2 us
  matrix products: 27.2 us -> 32.2 us
    psum x1 -> x0, waiting for transfers between devices: 136 us -> none  [local(): lax.psum(partial_grads.astype(jnp.bfloat16), 'config').astype(jnp.float32)]
    unnamed x3, waiting for transfers between devices: 106 us -> 78.7 us
    reduce_sum x0 -> x1, other arithmetic: none -> 4.19 us  [add_all(): total = pieces.sum(axis=0)]
  transfers between devices with their start and end apart: 6 -> 6, of which waited for: 4 -> 4; matrix products, arithmetic and copies ran while one was open for 7% -> 14% of each run, Pallas kernels for 0% -> 0%
where the time goes in v1:
time: 253 us; the launch traced here: 252 us
  waiting for transfers between devices  96.2 us (38%)
  local copies, waits for them, and re-layouts  37.9 us (15%)
  matrix products  32.2 us (13%)
  starting transfers between devices  30 us (12%)
  blocking collectives  24.1 us (10%)
  between operations  17.4 us (7%)
  other arithmetic  13.7 us (5%)
    unnamed x3, waiting for transfers between devices  78.7 us
    all_gather x1, blocking collectives, local(): lax.all_gather(local_hubs, 'graph', axis=1, tiled=True)  24.1 us
    all_to_all x1, starting transfers between devices, local(): lax.all_to_all(features.reshape(split_shape), 'config', split_axis=1, con...  10.5 us
    all_to_all x1, starting transfers between devices, local(): lax.all_to_all(aggregate.reshape(split_shape), 'config', split_axis=1, co...  9.81 us
    all_to_all x1, waiting for transfers between devices, local(): lax.all_to_all(aggregate.reshape(split_shape), 'config', split_axis=1, co...  8.94 us
    all_to_all x1, waiting for transfers between devices, local(): lax.all_to_all(aggr_node.reshape(back_shape), 'config', split_axis=0, con...  8 us
    dot_general x3, matrix products, attend(): jnp.einsum('khlm,mkhd->lkhd', attention, value_b, preferred_element_type=...  7.03 us
    dot_general x6, matrix products, project_back(): return jnp.dot(flat_rows, weight.T, preferred_element_type=jnp.float32)  6.9 us
  transfers between devices with their start and end apart: 6, of which 4 were waited for; matrix products, arithmetic and copies ran while one was open for 14% of the time, Pallas kernels for 0%

profile of v1, /device:TPU:1, one launch (start us, length us, event | category | flops | bytes accessed | tf_op | source)
XLA Modules:
  0.0 251.5 jit_solution(9683892311877536994)
XLA Ops:
  8.0 1.7 copy.113
  9.7 10.5 %all-to-all-start = ((bf16[2,32,16,128]{3,2,0,1:T(8,128)(2,1)}), bf16[2,32,16,128]{3,2,0,1:T(8,128)(2,1)S(1)}, u32[]{:S(2)}, u32[]{:S(2)}) async-start(bf16[2,32,16,128]{3,2,0,1:T(8,128)(2,1)} %copy.113), calls=%async_computation | async-start | bytes 524288 | tf_op jit(solution)/shard_map/all_to_all | solution.py:187
  20.2 0.7 compare_select_fusion
  20.9 0.7 compare_select_fusion.1
  21.6 1.5 gather_fusion.1
  23.8 0.7 compare_select_fusion.2
  24.4 1.6 gather_fusion
  26.1 1.6 multiply_bitcast_fusion.1
  27.7 1.9 copy.115
  29.6 1.8 scatter_fusion
  32.0 24.1 %all-gather = bf16[2,128,128]{2,1,0:T(8,128)(2,1)S(1)} all-gather(bf16[2,8,128]{2,1,0:T(8,128)(2,1)S(1)} %bitcast.206), channel_id=2, replica_groups=mesh['graph'=16,'config'=32] {'graph'}, dimensions={1}, use_global_device_ids=true | all-gather | bytes 69632 | tf_op jit(solution)/shard_map/all_gather | solution.py:178
  56.5 0.7 copy.118
  57.2 9.8 %all-to-all-start.1 = ((bf16[2,32,16,128]{3,2,0,1:T(8,128)(2,1)}), bf16[2,32,16,128]{3,2,0,1:T(8,128)(2,1)S(1)}, u32[]{:S(2)}, u32[]{:S(2)}) async-start(bf16[2,32,16,128]{3,2,0,1:T(8,128)(2,1)} %copy.118), calls=%async_computation.1 | async-start | bytes 524288 | tf_op jit(solution)/shard_map/all_to_all | solution.py:190
  67.7 1.8 copy.124
  69.8 8.9 %all-to-all-done.1 = bf16[2,32,16,128]{3,2,0,1:T(8,128)(2,1)S(1)} async-done(((bf16[2,32,16,128]{3,2,0,1:T(8,128)(2,1)}), bf16[2,32,16,128]{3,2,0,1:T(8,128)(2,1)S(1)}, u32[]{:S(2)}, u32[]{:S(2)}) %all-to-all-start.1) | async-done | bytes 262176 | tf_op jit(solution)/shard_map/all_to_all | solution.py:190
  78.7 1.0 multiply_convert_fusion
  80.2 1.0 convolution_convert_fusion.10
  81.6 1.2 copy.119
  83.2 1.2 copy.120
  84.4 2.2 fusion.7
  86.6 0.6 copy-done.17
  87.2 0.6 multiply_divide_fusion
  88.3 1.8 copy.121
  90.1 3.1 %fusion.6 = (f32[16,4,64]{2,1,0:T(4,128)S(1)}, bf16[16,4,64,64]{2,3,1,0:T(8,128)(2,1)S(1)}, bf16[16,4,64,64]{2,3,1,0:T(8,128)(2,1)S(1)}) fusion(f32[16,4,64,64]{2,3,1,0:T(8,128)} %get-tuple-element.20, f32[16,4,64]{2,1,0:T(4,128)} %multiply_divide_fusion, f32[16,4,64]{2,1,0:T(4,128)} %copy-done.17, bf16[16,4,32,64]{3,2,1,0:T(8,128)(2,1)} %copy.124, ...), kind=kOutput, calls=%fused_computation.14 | convolution fusion | flops 18870272 | bytes 2670592 | tf_op jit(solution)/shard_map/transpose(jvp(khlm,mkhd->lkhd))/dot_general | solution.py:31
  93.2 1.0 fusion.4
  94.3 1.5 fusion.9
  95.7 1.2 fusion.8
  96.9 2.5 %copy.131 = bf16[64,16,4,32]{3,2,1,0:T(4,128)(2,1)S(1)} copy(bf16[64,16,4,32]{0,3,2,1:T(8,128)(2,1)} %fusion.9) | data formatting | bytes 524288 | tf_op jit(solution)/shard_map/transpose(jvp(lkhd,mkhd->khlm))/convert_element_type | solution.py:24
  100.0 2.5 %copy.128 = bf16[64,16,4,32]{3,2,1,0:T(4,128)(2,1)S(1)} copy(bf16[64,16,4,32]{0,3,2,1:T(8,128)(2,1)} %fusion.8) | data formatting | bytes 524288 | tf_op jit(solution)/shard_map/transpose(jvp(lkhd,mkhd->khlm))/convert_element_type | solution.py:24
  102.5 1.2 reshape.192
  103.7 2.0 convolution_add_fusion.2
  105.7 2.5 fusion.10
  108.2 2.7 %copy.134 = bf16[64,16,4,32]{3,2,1,0:T(4,128)(2,1)S(1)} copy(bf16[64,16,4,32]{0,3,2,1:T(8,128)(2,1)} %fusion.10) | data formatting | bytes 524288 | tf_op jit(solution)/shard_map/transpose(jvp(khlm,mkhd->lkhd))/convert_element_type | solution.py:31
  111.0 1.2 reshape.194
  112.2 1.3 convolution_add_fusion.1
  113.5 1.5 fusion.18
  115.1 0.9 fusion.24
  116.0 0.9 convolution_convert_fusion.5
  116.9 0.9 fusion.26
  117.8 0.9 fusion.28
  118.7 0.9 fusion.30
  119.6 4.5 %all-to-all-start.3 = ((bf16[64,1,16,128]{3,2,1,0:T(8,128)(2,1)}), bf16[64,1,16,128]{3,2,1,0:T(8,128)(2,1)S(1)}, u32[]{:S(2)}, u32[]{:S(2)}) async-start(bf16[64,1,16,128]{3,2,1,0:T(8,128)(2,1)} %bitcast.37), calls=%async_computation.3 | async-start | bytes 524288 | tf_op jit(solution)/shard_map/all_to_all | solution.py:209
  124.1 0.9 fusion.32
  125.0 1.5 convolution_convert_fusion.4
  126.5 8.0 %all-to-all-done.3 = bf16[64,1,16,128]{3,2,1,0:T(8,128)(2,1)S(1)} async-done(((bf16[64,1,16,128]{3,2,1,0:T(8,128)(2,1)}), bf16[64,1,16,128]{3,2,1,0:T(8,128)(2,1)S(1)}, u32[]{:S(2)}, u32[]{:S(2)}) %all-to-all-start.3) | async-done | bytes 262176 | tf_op jit(solution)/shard_map/all_to_all | solution.py:209
  134.8 0.8 copy.145
  135.6 1.0 fusion.22
  136.6 1.7 copy.153
  138.4 1.3 dynamic-slice
  140.3 0.9 convolution_convert_fusion.6
  141.2 5.2 %all-to-all-start.2 = ((bf16[64,1,16,128]{3,2,1,0:T(8,128)(2,1)}), bf16[64,1,16,128]{3,2,1,0:T(8,128)(2,1)S(1)}, u32[]{:S(2)}, u32[]{:S(2)}) async-start(bf16[64,1,16,128]{3,2,1,0:T(8,128)(2,1)} %bitcast.32), calls=%async_computation.2 | async-start | bytes 524288 | tf_op jit(solution)/shard_map/all_to_all | solution.py:206
  146.4 1.6 copy.123
  148.6 1.7 fusion.13
  150.3 0.7 gather_fusion.2
  151.0 1.6 multiply_bitcast_fusion
  152.5 1.9 copy.140
  154.5 1.8 scatter_fusion.1
  157.1 0.6 bitcast_add_fusion
  157.7 78.7 %all-reduce.3.cloned.1.call-done = bf16[128,2,128]{2,1,0:T(2,128)(2,1)} async-done(((bf16[128,2,128]{2,1,0:T(2,128)(2,1)}), bf16[128,2,128]{2,1,0:T(2,128)(2,1)}) %all-reduce.3.cloned.1.call-update) | async-done | bytes 65552
  236.4 0.7 dynamic-slice_convert_fusion
  237.0 0.8 scatter_fusion.2
  238.0 0.7 copy.155
  238.8 4.2 %reduce_sum.40 = bf16[6,128,128]{2,1,0:T(8,128)(2,1)S(1)} reduce(bf16[32,6,128,128]{3,2,1,0:T(8,128)(2,1)} %all-gather.3.cloned.1.call-done, bf16[]{:T(256)} %constant.35.clone.1), dimensions={0}, to_apply=%region_6.7 | reduce | flops 3047424 | bytes 6488066 | tf_op jit(solution)/shard_map/reduce_sum | solution.py:13
  243.2 0.9 copy.156
  (75 shorter events, 6.1 us)
Async XLA Ops:
  8.0 18.1 %copy-start = (bf16[12,128,128]{2,1,0:T(8,128)(2,1)S(1)}, bf16[12,128,128]{2,1,0:T(8,128)(2,1)}, u32[]{:S(2)}) copy-start(bf16[12,128,128]{2,1,0:T(8,128)(2,1)} %param.14) | copy-start | bytes 1179652
  9.7 47.5 %all-to-all-start = ((bf16[2,32,16,128]{3,2,0,1:T(8,128)(2,1)}), bf16[2,32,16,128]{3,2,0,1:T(8,128)(2,1)S(1)}, u32[]{:S(2)}, u32[]{:S(2)}) async-start(bf16[2,32,16,128]{3,2,0,1:T(8,128)(2,1)} %copy.113), calls=%async_computation | async-start | bytes 524288 | tf_op jit(solution)/shard_map/all_to_all | solution.py:187
  27.7 1.9 copy-start.19
  31.5 24.6 %copy-start.11 = (bf16[512,128]{1,0:T(8,128)(2,1)S(1)}, bf16[512,128]{1,0:T(8,128)(2,1)}, u32[]{:S(2)}) copy-start(bf16[512,128]{1,0:T(8,128)(2,1)} %param.19) | copy-start | bytes 393220
  31.7 35.3 %copy-start.1 = (bf16[64,16,128]{2,1,0:T(8,128)(2,1)S(1)}, bf16[64,16,128]{2,1,0:T(8,128)(2,1)}, u32[]{:S(2)}) copy-start(bf16[64,16,128]{2,1,0:T(8,128)(2,1)} %param.11) | copy-start | bytes 786436
  31.7 35.3 %copy-start.13 = (bf16[4,128,128]{2,1,0:T(8,128)(2,1)S(1)}, bf16[4,128,128]{2,1,0:T(8,128)(2,1)}, u32[]{:S(2)}) copy-start(bf16[4,128,128]{2,1,0:T(8,128)(2,1)} %param.13) | copy-start | bytes 393220
  57.2 12.3 %copy-start.14 = (bf16[2,128,128]{2,1,0:T(8,128)(2,1)S(1)}, bf16[2,128,128]{2,1,0:T(8,128)(2,1)}, u32[]{:S(2)}) copy-start(bf16[2,128,128]{2,1,0:T(8,128)(2,1)} %param.12) | copy-start | bytes 196612
  57.2 21.5 %all-to-all-start.1 = ((bf16[2,32,16,128]{3,2,0,1:T(8,128)(2,1)}), bf16[2,32,16,128]{3,2,0,1:T(8,128)(2,1)S(1)}, u32[]{:S(2)}, u32[]{:S(2)}) async-start(bf16[2,32,16,128]{3,2,0,1:T(8,128)(2,1)} %copy.118), calls=%async_computation.1 | async-start | bytes 524288 | tf_op jit(solution)/shard_map/all_to_all | solution.py:190
  78.7 2.4 copy-start.9
  82.8 3.8 %copy-start.4 = (bf16[64,16,4,32]{0,3,2,1:T(8,128)(2,1)}, bf16[64,16,4,32]{0,3,2,1:T(8,128)(2,1)S(1)}, u32[]{:S(2)}) copy-start(bf16[64,16,4,32]{0,3,2,1:T(8,128)(2,1)S(1)} %copy.119) | copy-start | bytes 786436
  84.4 3.9 %copy-start.6 = (bf16[64,16,4,32]{0,3,2,1:T(8,128)(2,1)}, bf16[64,16,4,32]{0,3,2,1:T(8,128)(2,1)S(1)}, u32[]{:S(2)}) copy-start(bf16[64,16,4,32]{0,3,2,1:T(8,128)(2,1)S(1)} %copy.120) | copy-start | bytes 786436
  86.6 0.6 copy-start.17
  90.1 3.1 %copy-start.3 = (f32[16,4,64,64]{2,3,1,0:T(8,128)S(1)}, f32[16,4,64,64]{2,3,1,0:T(8,128)}, u32[]{:S(2)}) copy-start(f32[16,4,64,64]{2,3,1,0:T(8,128)} %get-tuple-element.20) | copy-start | bytes 3145732
  90.1 3.1 %copy-start.18 = (f32[16,4,64]{2,1,0:T(4,128)S(1)}, f32[16,4,64]{2,1,0:T(4,128)}, u32[]{:S(2)}) copy-start(f32[16,4,64]{2,1,0:T(4,128)} %copy-done.17) | copy-start | bytes 49156
  93.2 1.0 copy-start.5
  94.3 1.5 copy-start.7
  113.5 2.5 copy-start.15
  113.5 3.4 %copy-start.10 = (bf16[2,32,16,128]{3,2,0,1:T(8,128)(2,1)S(1)}, bf16[2,32,16,128]{3,2,0,1:T(8,128)(2,1)}, u32[]{:S(2)}) copy-start(bf16[2,32,16,128]{3,2,0,1:T(8,128)(2,1)} %copy-done.9) | copy-start | bytes 786436
  113.5 4.3 %copy-start.2 = (bf16[1024,128]{1,0:T(8,128)(2,1)S(1)}, bf16[1024,128]{1,0:T(8,128)(2,1)}, u32[]{:S(2)}) copy-start(bf16[1024,128]{1,0:T(8,128)(2,1)} %reshape.192) | copy-start | bytes 786436
  115.1 9.0 %copy-start.8 = (bf16[1024,128]{1,0:T(8,128)(2,1)S(1)}, bf16[1024,128]{1,0:T(8,128)(2,1)}, u32[]{:S(2)}) copy-start(bf16[1024,128]{1,0:T(8,128)(2,1)} %reshape.194) | copy-start | bytes 786436
  119.6 14.9 %copy-start.12 = (bf16[512,128]{1,0:T(8,128)(2,1)S(1)}, bf16[512,128]{1,0:T(8,128)(2,1)}, u32[]{:S(2)}) copy-start(bf16[512,128]{1,0:T(8,128)(2,1)} %param.19) | copy-start | bytes 393220
  119.6 14.9 %all-to-all-start.3 = ((bf16[64,1,16,128]{3,2,1,0:T(8,128)(2,1)}), bf16[64,1,16,128]{3,2,1,0:T(8,128)(2,1)S(1)}, u32[]{:S(2)}, u32[]{:S(2)}) async-start(bf16[64,1,16,128]{3,2,1,0:T(8,128)(2,1)} %bitcast.37), calls=%async_computation.3 | async-start | bytes 524288 | tf_op jit(solution)/shard_map/all_to_all | solution.py:209
  124.1 112.3 %all-reduce.3.cloned.1.call-start = ((), (), s32[]{:S(2)}) async-start(), calls=%async_computation.5 | async-start | bytes 131072
  125.0 15.3 %copy-start.16 = (bf16[2,128,128]{2,1,0:T(8,128)(2,1)S(1)}, bf16[2,128,128]{2,1,0:T(8,128)(2,1)}, u32[]{:S(2)}) copy-start(bf16[2,128,128]{2,1,0:T(8,128)(2,1)} %param.12) | copy-start | bytes 196612
  135.6 103.2 %all-gather.3.cloned.1.call-start = ((), (), s32[]{:S(2)}) async-start(), calls=%async_computation.4 | async-start | bytes 6488064 | tf_op jit(solution)/shard_map/all_gather | solution.py:12
  141.2 15.6 %all-to-all-start.2 = ((bf16[64,1,16,128]{3,2,1,0:T(8,128)(2,1)}), bf16[64,1,16,128]{3,2,1,0:T(8,128)(2,1)S(1)}, u32[]{:S(2)}, u32[]{:S(2)}) async-start(bf16[64,1,16,128]{3,2,1,0:T(8,128)(2,1)} %bitcast.32), calls=%async_computation.2 | async-start | bytes 524288 | tf_op jit(solution)/shard_map/all_to_all | solution.py:206
  152.5 1.9 copy-start.20
Sparse Core Ops, SparseCore 0:
  135.7 100.6 all-reduce.2
Sparse Core Ops, SparseCore 1:
  140.3 86.5 all-gather.2
